TPU v7x, 32 devices: a whole 2x2x4 slice. The times are simulated.
32 devices in a mesh: tok: 2 (over y), feat: 16 (over z, x, core).
Axes of the slice: x: 2, y: 2, z: 4, core: 2. Of those that a mesh axis runs over, the one named last changes fastest.
Arguments:
- tokens: bfloat16 [256, 4096], P('tok', 'feat'), may hold values from -6 to 6
- seq_lengths: int32 [4], replicated, may hold values from 1 to 64, 128 in all
- in_exponents: int32 [4096], replicated, may hold values from -1 to 1
- hidden_exponents: int32 [16384], P('feat'), may hold values from -2 to 0
- gateup_blocks: int32 [128, 16], P('feat'), may hold values from 0 to 31, as said below
- down_blocks: int32 [128, 16], P('feat'), may hold values from 0 to 31, as said below
- gate_values: bfloat16 [128, 16, 128, 128], P('feat', 'tok'), may hold values from -0.125 to 0.125
- up_values: bfloat16 [128, 16, 128, 128], P('feat', 'tok'), may hold values from -0.125 to 0.125
- down_values: bfloat16 [128, 16, 128, 128], P('feat', 'tok'), may hold values from -0.25 to 0.25
Outputs:
- ffn_output: bfloat16 [256, 4096], P('tok', 'feat')
Inputs may be any that keep to these rules, and one draw needn't show every extreme that they name: `seq_lengths`: the lengths add up to 128; sequence q fills the token slots from q * 64 on, the rest of its 64 slots is empty. `gateup_blocks`: each row holds 16 different block numbers in rising order. `down_blocks`: each row holds 16 different block numbers in rising order.
All inputs are finite; a program needn't handle non-finite values.
Results may differ from a plain program's by a relative error of at most 0.0057.
Values may be sent and summed in bfloat16 or wider, within the bound.
A program may use at most 128 MiB of HBM per device.

v0:
```python
import math

import jax
import jax.numpy as jnp
from jax import lax
from jax.sharding import PartitionSpec as P

TIME_STEPS = 4
SEQS_DEV = 2


def partner_2(value, axis, stride):
    mask = 2**stride
    pairs = [(source, source ^ mask) for source in range(lax.axis_size(axis))]
    return lax.ppermute(value, axis, pairs)


def sign_table(order_size, value_type):
    indices = jnp.arange(order_size, dtype=jnp.int32)
    shared = indices[:, None] & indices[None, :]
    parity = jnp.zeros((order_size, order_size), jnp.int32)
    for bit_number in range(max(1, (order_size - 1).bit_length())):
        parity = parity ^ shared >> bit_number & 1
    return (1 - 2 * parity).astype(value_type)


def local(
    tokens,
    seq_lengths,
    in_exponents,
    hidden_exponents,
    gateup_blocks,
    down_blocks,
    gate_values,
    up_values,
    down_values,
):
    slot_count, feat_local = tokens.shape
    model_width = in_exponents.shape[0]
    seq_width = slot_count // SEQS_DEV
    tok_index = lax.axis_index("tok")
    seq_ends = jnp.cumsum(seq_lengths)
    seq_starts = seq_ends - seq_lengths
    seq_ids = jnp.arange(seq_lengths.shape[0], dtype=jnp.int32)
    slot_ids = jnp.arange(slot_count, dtype=jnp.int32)
    seq_of = tok_index * SEQS_DEV + slot_ids // seq_width
    position = slot_ids % seq_width
    same_seq = seq_of[:, None] == seq_ids[None, :]
    length_of = jnp.sum(jnp.where(same_seq, seq_lengths[None, :], 0), axis=1)
    start_of = jnp.sum(jnp.where(same_seq, seq_starts[None, :], 0), axis=1)
    live_slot = position < length_of
    pooled = lax.all_gather(tokens, "tok", axis=0, tiled=True)
    wanted = tok_index * seq_width + jnp.arange(seq_width, dtype=jnp.int32)
    owner_seq = jnp.sum((seq_ends[None, :] <= wanted[:, None]).astype(jnp.int32), axis=1)
    owner_match = owner_seq[:, None] == seq_ids[None, :]
    offset = wanted - jnp.sum(jnp.where(owner_match, seq_starts[None, :], 0), axis=1)
    picked = jnp.take(pooled, owner_seq * seq_width + offset, axis=0)
    row_count = picked.shape[0]
    rotation_scale = 1.0 / math.sqrt(model_width)
    mixed_part = jnp.dot(
        picked, sign_table(feat_local, jnp.bfloat16), preferred_element_type=jnp.float32
    )
    feat_index = lax.axis_index("feat")
    for bit_number in range(lax.axis_size("feat").bit_length() - 1):
        partner = partner_2(mixed_part, "feat", bit_number)
        high_half = feat_index >> bit_number & 1 == 1
        mixed_part = jnp.where(high_half, partner - mixed_part, mixed_part + partner)
    rotated = lax.all_gather(
        (mixed_part * rotation_scale).astype(jnp.bfloat16), "feat", axis=1, tiled=True
    )
    in_limit = jnp.exp2(in_exponents.astype(jnp.float32))
    hidden_limit = jnp.exp2(hidden_exponents.astype(jnp.float32))
    gate_full, up_full, down_full = (
        lax.all_gather(gate_values, "tok", axis=1, tiled=True),
        lax.all_gather(up_values, "tok", axis=1, tiled=True),
        lax.all_gather(down_values, "tok", axis=1, tiled=True),
    )
    block_size = gate_values.shape[2]
    block_count = model_width // block_size
    hidden_local = hidden_exponents.shape[0]
    v_in = jnp.zeros((row_count, model_width), jnp.float32)
    v_hidden = jnp.zeros((row_count, hidden_local), jnp.float32)
    spike_count_sum = jnp.zeros((row_count, hidden_local), jnp.float32)
    for step_index in range(TIME_STEPS):
        v_in = v_in + rotated.astype(jnp.float32)
        spike_in = jnp.clip(v_in, -in_limit, in_limit).astype(jnp.bfloat16)
        v_in = v_in - spike_in.astype(jnp.float32)
        chosen = jnp.take(
            spike_in.reshape(row_count, block_count, block_size), gateup_blocks, axis=1
        )
        gate_sum = jnp.einsum(
            "rhkb,hkbc->rhc", chosen, gate_full, preferred_element_type=jnp.float32
        )
        upward = jnp.einsum("rhkb,hkbc->rhc", chosen, up_full, preferred_element_type=jnp.float32)
        current = (jax.nn.silu(gate_sum) * upward).reshape(row_count, hidden_local)
        v_hidden = v_hidden + current
        spike_hidden = jnp.clip(v_hidden, -hidden_limit, hidden_limit)
        v_hidden = v_hidden - spike_hidden
        spike_count_sum = spike_count_sum + spike_hidden
    spiking_rate = (spike_count_sum / TIME_STEPS).astype(jnp.bfloat16)
    indicator = (
        down_blocks[:, :, None] == jnp.arange(block_count, dtype=jnp.int32)[None, None, :]
    ).astype(jnp.bfloat16)
    dense_down_weight = jnp.einsum(
        "hkbc,hkn->hbnc", down_full, indicator, preferred_element_type=jnp.float32
    ).astype(jnp.bfloat16)
    dense_down_weight = dense_down_weight.reshape(hidden_local, model_width)
    partial_block_value = jnp.dot(
        spiking_rate, dense_down_weight, preferred_element_type=jnp.float32
    )
    summed = lax.psum_scatter(partial_block_value, "feat", scatter_dimension=1, tiled=True)
    returned = lax.all_gather(summed.astype(jnp.bfloat16), "tok", axis=0, tiled=True)
    source_row = jnp.where(live_slot, start_of + position, 0)
    result_rows = jnp.take(returned, source_row, axis=0)
    return jnp.where(live_slot[:, None], result_rows, jnp.zeros_like(result_rows))


def solution(mesh):
    in_specs = (
        P("tok", "feat"),
        P(),
        P(),
        P("feat"),
        P("feat", None),
        P("feat", None),
        P("feat", "tok", None, None),
        P("feat", "tok", None, None),
        P("feat", "tok", None, None),
    )
    out_specs = P("tok", "feat")
    return jax.shard_map(local, mesh=mesh, in_specs=in_specs, out_specs=out_specs, check_vma=False)
```

profile of v0, /device:TPU:0, one launch (start us, length us, event | category | flops | bytes accessed | tf_op | source)
XLA Modules:
  0.0 264.7 jit_solution(782521397529941835)
XLA Ops:
  8.3 5.9 %all_gather.18 = bf16[256,256]{1,0:T(8,128)(2,1)S(1)} all-gather(bf16[128,256]{1,0:T(8,128)(2,1)S(1)} %copy-done.5), channel_id=1, replica_groups=mesh['tok'=2,'feat'=16] {'tok'}, dimensions={0}, use_global_device_ids=true | all-gather | bytes 196608 | tf_op jit(solution)/shard_map/all_gather | solution.py:52
  15.4 2.8 %copy.26 = bf16[8,8,128,128]{3,1,2,0:T(8,128)(2,1)} copy(bf16[8,8,128,128]{3,2,1,0:T(8,128)(2,1)S(1)} %copy-done.4) | data formatting | bytes 4194304 | tf_op args[8]
  19.0 2.1 collective-permute-start.1
  21.1 2.8 %collective-permute-done.1 = f32[64,256]{1,0:T(8,128)S(1)} collective-permute-done((f32[64,256]{1,0:T(8,128)S(1)}, f32[64,256]{1,0:T(8,128)S(1)}, u32[]{:S(2)}, u32[]{:S(2)}) %collective-permute-start.1) | collective-permute-done | bytes 65568 | tf_op jit(solution)/shard_map/ppermute | solution.py:15
  23.8 1.9 collective-permute-start.2
  25.8 2.4 collective-permute-done.2
  28.2 2.9 %collective-permute-start.3 = (f32[64,256]{1,0:T(8,128)S(1)}, f32[64,256]{1,0:T(8,128)S(1)}, u32[]{:S(2)}, u32[]{:S(2)}) collective-permute-start(f32[64,256]{1,0:T(8,128)S(1)} %add_select_fusion), channel_id=1, source_target_pairs={{0,8},{1,9},{2,10},{3,11},{4,12},{5,13},{6,14},{7,15},{8,0},{9,1},... | collective-permute-start | bytes 196616 | tf_op jit(solution)/shard_map/ppermute | solution.py:15
  31.1 2.4 collective-permute-done.3
  33.5 24.2 %all_gather.19 = bf16[64,4096]{1,0:T(8,128)(2,1)S(1)} all-gather(bf16[64,256]{1,0:T(8,128)(2,1)S(1)} %multiply_convert_fusion), channel_id=1, replica_groups=mesh['tok'=2,'feat'=16] {'feat'}, dimensions={1}, use_global_device_ids=true | all-gather | bytes 557056 | tf_op jit(solution)/shard_map/all_gather | solution.py:68
  57.7 1.6 fusion.95
  59.6 2.1 gather_fusion.2
  61.7 0.9 gather_fusion.3
  62.7 1.5 copy_bitcast_fusion
  64.2 2.1 gather_fusion.4
  66.3 2.1 gather_fusion.5
  68.5 3.9 %fusion.19 = f32[64,8,128]{2,0,1:T(8,128)S(1)} fusion(bf16[8,16,128,128]{3,2,1,0:T(8,128)(2,1)} %all-gather.4.cloned.1.call-done, bf16[8,16,64,128]{3,2,1,0:T(8,128)(2,1)} %bitcast.205, pred[8,16]{1,0:T(8,128)(4,1)S(1)} %compare_and_fusion), kind=kOutput, calls=%fused_computation.35 | convolution fusion | flops 269484032 | bytes 6553728 | tf_op jit(solution)/shard_map/rhkb,hkbc->rhc/dot_general | solution.py:91
  72.5 1.0 fusion.25
  74.1 1.0 fusion.31
  75.7 1.0 fusion.37
  76.7 50.0 %all-gather.6.cloned.1.call-done = bf16[8,16,128,128]{3,2,1,0:T(8,128)(2,1)} async-done(((bf16[8,8,128,128]{3,2,1,0:T(8,128)(2,1)}), bf16[8,16,128,128]{3,2,1,0:T(8,128)(2,1)}) %all-gather.6.cloned.1.call-update) | async-done | bytes 4194320 | tf_op jit(solution)/shard_map/all_gather | solution.py:75
  126.7 4.0 %fusion.61 = f32[64,8,128]{2,0,1:T(8,128)S(1)} fusion(bf16[8,16,128,128]{3,2,1,0:T(8,128)(2,1)} %all-gather.6.cloned.1.call-done, bf16[8,16,64,128]{3,2,1,0:T(8,128)(2,1)} %bitcast.206, pred[8,16]{1,0:T(8,128)(4,1)S(1)} %compare_and_fusion, f32[64,8,128]{2,0,1:T(8,128)S(1)} %fusion.19), kind=kOutput, calls=%fused_computation.49 | convolution fusion | flops 269811712 | bytes 6815872 | tf_op jit(solution)/shard_map/rhkb,hkbc->rhc/dot_general | solution.py:94
  130.7 1.1 fusion.58
  132.3 1.0 fusion.52
  133.9 1.1 fusion.79
  135.0 50.0 %all-gather.8.cloned.1.call-done = bf16[8,16,128,128]{3,1,2,0:T(8,128)(2,1)} async-done(((bf16[8,8,128,128]{3,1,2,0:T(8,128)(2,1)}), bf16[8,16,128,128]{3,1,2,0:T(8,128)(2,1)}) %all-gather.8.cloned.1.call-update) | async-done | bytes 4194320 | tf_op jit(solution)/shard_map/all_gather | solution.py:76
  185.0 4.9 %convolution_convert_fusion = bf16[8,32,128,128]{3,1,2,0:T(8,128)(2,1)S(1)} fusion(bf16[8,16,128,128]{3,1,2,0:T(8,128)(2,1)} %all-gather.8.cloned.1.call-done, s32[8,16]{1,0:T(8,128)S(1)} %copy-done.8), kind=kOutput, calls=%fused_computation.9 | convolution fusion | flops 138416128 | bytes 12583424 | tf_op jit(solution)/shard_map/hkbc,hkn->hbnc/dot_general | solution.py:104
  189.9 3.7 %fusion = f32[64,4096]{1,0:T(8,128)} fusion(bf16[128,8,32,128]{3,2,1,0:T(8,128)(2,1)S(1)} %bitcast.202, bf16[8,8,8,128]{3,2,1,0:T(8,128)(2,1)S(1)} %fusion.79), kind=kOutput, calls=%fused_computation.6 | convolution fusion | flops 536870912 | bytes 9568256 | tf_op jit(solution)/shard_map/dot_general | solution.py:108
  193.8 57.4 %reduce-scatter.2.cloned.1.call-done = f32[64,256]{1,0:T(8,128)} async-done(((f32[64,4096]{1,0:T(8,128)}), f32[64,256]{1,0:T(8,128)}) %reduce-scatter.2.cloned.1.call-update) | async-done | bytes 65552 | tf_op jit(solution)/shard_map/reduce_scatter | solution.py:111
  251.1 0.8 convert_element_type.75
  252.0 4.6 %all_gather.23 = bf16[128,256]{1,0:T(8,128)(2,1)S(1)} all-gather(bf16[64,256]{1,0:T(8,128)(2,1)S(1)} %convert_element_type.75), channel_id=1, replica_groups=mesh['tok'=2,'feat'=16] {'tok'}, dimensions={0}, use_global_device_ids=true | all-gather | bytes 98304 | tf_op jit(solution)/shard_map/all_gather | solution.py:112
  256.6 0.8 gather_fusion.1
  257.4 0.7 select_select_fusion
  (63 shorter events, 6.6 us)
Async XLA Ops:
  6.5 1.5 copy-start.10
  6.5 1.7 copy-start.5
  6.5 61.9 %all-gather.4.cloned.1.call-start = ((), (), s32[]{:S(2)}) async-start(), calls=%async_computation.1 | async-start | bytes 6291456 | tf_op jit(solution)/shard_map/all_gather | solution.py:74
  7.3 8.1 %copy-start.4 = (bf16[8,8,128,128]{3,2,1,0:T(8,128)(2,1)S(1)}, bf16[8,8,128,128]{3,2,1,0:T(8,128)(2,1)}, u32[]{:S(2)}) copy-start(bf16[8,8,128,128]{3,2,1,0:T(8,128)(2,1)} %param.19) | copy-start | bytes 6291460
  7.3 119.4 %all-gather.6.cloned.1.call-start = ((), (), s32[]{:S(2)}) async-start(), calls=%async_computation.2 | async-start | bytes 6291456 | tf_op jit(solution)/shard_map/all_gather | solution.py:75
  8.0 177.0 %all-gather.8.cloned.1.call-start = ((), (), s32[]{:S(2)}) async-start(), calls=%async_computation.3 | async-start | bytes 6291456 | tf_op jit(solution)/shard_map/all_gather | solution.py:76
  15.4 3.5 %collective-permute-start = (f32[64,256]{1,0:T(8,128)S(1)}, f32[64,256]{1,0:T(8,128)S(1)}, u32[]{:S(2)}, u32[]{:S(2)}) collective-permute-start(f32[64,256]{1,0:T(8,128)S(1)} %fusion.98), channel_id=1, source_target_pairs={{0,1},{1,0},{2,3},{3,2},{4,5},{5,4},{6,7},{7,6},{8,9},{9,8},{10,11... | collective-permute-start | bytes 196616 | tf_op jit(solution)/shard_map/ppermute | solution.py:15
  18.2 0.7 copy-start.7
  18.2 0.7 copy-start.9
  18.2 2.9 %copy-start.6 = (s32[8,16]{1,0:T(8,128)S(1)}, s32[8,16]{1,0:T(8,128)}, u32[]{:S(2)}) copy-start(s32[8,16]{1,0:T(8,128)} %param.15) | copy-start | bytes 1540
  18.2 232.9 %reduce-scatter.2.cloned.1.call-start = ((), (), s32[]{:S(2)}) async-start(), calls=%async_computation.4 | async-start | bytes 1114112 | tf_op jit(solution)/shard_map/reduce_scatter | solution.py:111
  19.0 4.8 %collective-permute-start.1 = (f32[64,256]{1,0:T(8,128)S(1)}, f32[64,256]{1,0:T(8,128)S(1)}, u32[]{:S(2)}, u32[]{:S(2)}) collective-permute-start(f32[64,256]{1,0:T(8,128)S(1)} %add_select_fusion.2), channel_id=1, source_target_pairs={{0,2},{1,3},{2,0},{3,1},{4,6},{5,7},{6,4},{7,5},{8,10},{9,11},{10,... | collective-permute-start | bytes 196616 | tf_op jit(solution)/shard_map/ppermute | solution.py:15
  23.8 4.3 %collective-permute-start.2 = (f32[64,256]{1,0:T(8,128)S(1)}, f32[64,256]{1,0:T(8,128)S(1)}, u32[]{:S(2)}, u32[]{:S(2)}) collective-permute-start(f32[64,256]{1,0:T(8,128)S(1)} %add_select_fusion.1), channel_id=1, source_target_pairs={{0,4},{1,5},{2,6},{3,7},{4,0},{5,1},{6,2},{7,3},{8,12},{9,13},{10,... | collective-permute-start | bytes 196616 | tf_op jit(solution)/shard_map/ppermute | solution.py:15
  28.2 5.3 %collective-permute-start.3 = (f32[64,256]{1,0:T(8,128)S(1)}, f32[64,256]{1,0:T(8,128)S(1)}, u32[]{:S(2)}, u32[]{:S(2)}) collective-permute-start(f32[64,256]{1,0:T(8,128)S(1)} %add_select_fusion), channel_id=1, source_target_pairs={{0,8},{1,9},{2,10},{3,11},{4,12},{5,13},{6,14},{7,15},{8,0},{9,1},... | collective-permute-start | bytes 196616 | tf_op jit(solution)/shard_map/ppermute | solution.py:15
  68.5 4.0 %copy-start.12 = (bf16[8,16,128,128]{3,2,1,0:T(8,128)(2,1)S(1)}, bf16[8,16,128,128]{3,2,1,0:T(8,128)(2,1)}, u32[]{:S(2)}) copy-start(bf16[8,16,128,128]{3,2,1,0:T(8,128)(2,1)} %all-gather.4.cloned.1.call-done) | copy-start | bytes 12582916
  72.5 1.6 copy-start.2
  74.1 1.6 copy-start
  126.7 4.0 %copy-start.11 = (bf16[8,16,128,128]{3,2,1,0:T(8,128)(2,1)S(1)}, bf16[8,16,128,128]{3,2,1,0:T(8,128)(2,1)}, u32[]{:S(2)}) copy-start(bf16[8,16,128,128]{3,2,1,0:T(8,128)(2,1)} %all-gather.6.cloned.1.call-done) | copy-start | bytes 12582916
  130.7 1.6 copy-start.3
  132.3 1.6 copy-start.1
  133.9 51.1 %copy-start.8 = (s32[8,16]{1,0:T(8,128)S(1)}, s32[8,16]{1,0:T(8,128)}, u32[]{:S(2)}) copy-start(s32[8,16]{1,0:T(8,128)} %param.16) | copy-start | bytes 1540
Sparse Core Ops, SparseCore 0:
  8.9 59.4 all-gather.3
  69.9 56.7 all-gather.5
  128.3 56.7 all-gather.7
  193.8 57.3 reduce-scatter.1
where the time goes:
time: 265 us
  waiting for transfers between devices  166 us (63%)
  blocking collectives  34.6 us (13%)
  matrix products  23.1 us (9%)
  local copies, waits for them, and re-layouts  16.5 us (6%)
  between operations  13.3 us (5%)
  starting transfers between devices  6.99 us (3%)
  other arithmetic  3.82 us (1%)
    reduce_scatter x1, waiting for transfers between devices, local(): lax.psum_scatter(partial_block_value, 'feat', scatter_dimension=1, tiled=...  57.4 us
    all_gather x1, waiting for transfers between devices, local(): lax.all_gather(up_values, 'tok', axis=1, tiled=True)  50 us
    all_gather x1, waiting for transfers between devices, local(): lax.all_gather(down_values, 'tok', axis=1, tiled=True)  50 us
    all_gather x1, blocking collectives, local(): lax.all_gather((mixed_part * rotation_scale).astype(jnp.bfloat16), 'feat'...  24.2 us
    ppermute x4, waiting for transfers between devices, partner_2(): return lax.ppermute(value, axis, pairs)  7.52 us
    gather x4, local copies, waits for them, and re-layouts, local(): jnp.take(spike_in.reshape(row_count, block_count, block_size), gateup_blo...  7.35 us
    dot_general x4, matrix products, local(): jnp.einsum('rhkb,hkbc->rhc', chosen, up_full, preferred_element_type=jnp....  7.15 us
    dot_general x4, matrix products, local(): jnp.einsum('rhkb,hkbc->rhc', chosen, gate_full, preferred_element_type=jn...  6.97 us
  transfers between devices with their start and end apart: 8, of which 6 were waited for; matrix products, arithmetic and copies ran while one was open for 11% of the time, Pallas kernels for 0%

commit v1 on v0

--- a/solution.py
+++ b/solution.py
@@ -2,11 +2,460 @@
 
 import jax
 import jax.numpy as jnp
+import numpy as np
 from jax import lax
+from jax.experimental import pallas as pl
+from jax.experimental.pallas import tpu as pltpu
 from jax.sharding import PartitionSpec as P
 
-TIME_STEPS = 4
 SEQS_DEV = 2
+MESH_ID = pl.DeviceIdType.MESH
+F32 = jnp.float32
+BF16 = jnp.bfloat16
+
+
+def slot_target(lengths, slots, seq_width):
+    seq = slots // seq_width
+    position = slots % seq_width
+    start = jnp.zeros_like(slots)
+    length = jnp.zeros_like(slots)
+    running = 0
+    for q, length_q in enumerate(lengths):
+        here = seq == q
+        start = jnp.where(here, running, start)
+        length = jnp.where(here, length_q, length)
+        running = running + length_q
+    return jnp.where(position < length, start + position, -1)
+
+
+def body(
+    lengths_ref,
+    gateup_ref,
+    slot_of_ref,
+    tok_ref,
+    in_exp_ref,
+    hid_exp_ref,
+    sign_ref,
+    gate_hbm,
+    up_hbm,
+    down_hbm,
+    out_ref,
+    gate,
+    up,
+    down,
+    peer_tok,
+    all_tok,
+    mixed,
+    in_limit,
+    spikes,
+    snd_gu,
+    rcv_gu,
+    rate,
+    snd_c,
+    rcv_c,
+    snd_x,
+    rcv_x,
+    acc,
+    snd_y,
+    rcv_y,
+    snd_z,
+    rcv_z,
+    final,
+    w_sem,
+    raw_s,
+    raw_r,
+    agz_s,
+    agz_r,
+    agx_s,
+    agx_r,
+    agc_s,
+    agc_r,
+    gu_s,
+    gu_r,
+    rt_s,
+    rt_r,
+    c_s,
+    c_r,
+    x_s,
+    x_r,
+    y_s,
+    y_r,
+    z_s,
+    z_r,
+    fin_s,
+    fin_r,
+):
+    t = lax.axis_index("tok")
+    f = lax.axis_index("feat")
+    z = f // 4
+    x = (f // 2) % 2
+    c = f % 2
+    slots, width = tok_ref.shape
+    live = slots
+    half = live // 2
+    side = slots // SEQS_DEV
+    columns = rate.shape[0]
+    mine = columns // 2
+    kk = gateup_ref.shape[1] // 2
+
+    dev_y = (1 - t, f)
+    dev_c = (t, f + 1 - 2 * c)
+    dev_x = (t, f + 2 - 4 * x)
+
+    def z_at(d):
+        return lax.rem(z + d, 4)
+
+    def dev_z(d):
+        return (t, z_at(d) * 4 + x * 2 + c)
+
+    def chunk(zz, xx, cc):
+        return zz * 4 + xx * 2 + cc
+
+    def send(src, dst, ssem, rsem, dev):
+        return pltpu.make_async_remote_copy(
+            src_ref=src,
+            dst_ref=dst,
+            send_sem=ssem,
+            recv_sem=rsem,
+            device_id=dev,
+            device_id_type=MESH_ID,
+        )
+
+    w_copies = [
+        pltpu.make_async_copy(gate_hbm, gate, w_sem.at[0]),
+        pltpu.make_async_copy(up_hbm, up, w_sem.at[1]),
+        pltpu.make_async_copy(down_hbm, down.at[:, pl.ds(1, kk)], w_sem.at[2]),
+    ]
+    for copy in w_copies:
+        copy.start()
+
+    barrier = pltpu.get_barrier_semaphore()
+    partners = [dev_y, dev_c, dev_x, dev_z(1), dev_z(2), dev_z(3)]
+    for dev in partners:
+        pl.semaphore_signal(barrier, inc=1, device_id=dev, device_id_type=MESH_ID)
+    pl.semaphore_wait(barrier, len(partners))
+
+    raw = send(tok_ref, peer_tok, raw_s.at[0], raw_r.at[0], dev_y)
+    raw.start()
+    down[:, pl.ds(0, 1)] = jnp.zeros((columns, 1) + down.shape[2:], BF16)
+    in_limit[...] = jnp.exp2(in_exp_ref[...].astype(F32)).astype(BF16).astype(F32)
+    lengths = [lengths_ref[q] for q in range(lengths_ref.shape[0])]
+    rows = lax.broadcasted_iota(jnp.int32, (live, slots), 0)
+    lane_slots = lax.broadcasted_iota(jnp.int32, (live, slots), 1)
+
+    def pick(group):
+        target = slot_target(lengths, lane_slots + group * slots, side)
+        return jnp.where(target == rows, 1.0, 0.0).astype(BF16)
+
+    own_rows = jnp.dot(pick(t), tok_ref[...], preferred_element_type=F32)
+    other_pick = pick(1 - t)
+    raw.wait_recv()
+    other_rows = jnp.dot(other_pick, peer_tok[...], preferred_element_type=F32)
+    all_tok[f] = (own_rows + other_rows).astype(BF16)
+
+    sent = [raw]
+
+    def start(copy):
+        copy.start()
+        sent.append(copy)
+        return copy
+
+    def rotate_low(g):
+        mixed[g] = jnp.dot(all_tok[g], sign_ref[...], preferred_element_type=F32)
+
+    def forward_x(d, g):
+        return start(send(all_tok.at[g], all_tok.at[g], agx_s.at[d], agx_r.at[d], dev_x))
+
+    def forward_c(d, g):
+        return start(send(all_tok.at[g], all_tok.at[g], agc_s.at[d], agc_r.at[d], dev_c))
+
+    z_copies = [
+        start(send(all_tok.at[f], all_tok.at[f], agz_s.at[d - 1], agz_r.at[d - 1], dev_z(d)))
+        for d in (1, 2, 3)
+    ]
+    x_copies = [forward_x(0, f)]
+    c_copies = [forward_c(0, f)]
+    rotate_low(f)
+    for d in (1, 3, 2):
+        z_copies[d - 1].wait_recv()
+        g = chunk(z_at(4 - d), x, c)
+        x_copies.append(forward_x(d, g))
+        c_copies.append(forward_c(d, g))
+        rotate_low(g)
+    for i, d in enumerate((0, 1, 3, 2)):
+        x_copies[i].wait_recv()
+        g = chunk(z_at(4 - d), 1 - x, c)
+        c_copies.append(forward_c(4 + d, g))
+        rotate_low(g)
+    for i, d in enumerate((0, 1, 3, 2)):
+        c_copies[i].wait_recv()
+        rotate_low(chunk(z_at(4 - d), x, 1 - c))
+    for i, d in enumerate((0, 1, 3, 2)):
+        c_copies[4 + i].wait_recv()
+        rotate_low(chunk(z_at(4 - d), 1 - x, 1 - c))
+
+    chunks = mixed.shape[0]
+    scale = 1.0 / math.sqrt(chunks * width)
+    parts = width // 128
+
+    def rotate_high(r, carry):
+        at = pl.ds(pl.multiple_of(r * 16, 16), 16)
+        for h in range(parts):
+            vals = [mixed[i, at, pl.ds(h * 128, 128)] for i in range(chunks)]
+            bit = 1
+            while bit < chunks:
+                nxt = list(vals)
+                for i in range(chunks):
+                    if not i & bit:
+                        nxt[i] = vals[i] + vals[i | bit]
+                        nxt[i | bit] = vals[i] - vals[i | bit]
+                vals = nxt
+                bit *= 2
+            for i in range(chunks):
+                n = parts * i + h
+                limit = in_limit[pl.ds(n, 1), :]
+                rotated = (vals[i] * scale).astype(BF16).astype(F32)
+                spikes[n, at, :] = jnp.minimum(jnp.maximum(rotated, -limit), limit).astype(BF16)
+        return carry
+
+    lax.fori_loop(0, live // 16, rotate_high, 0)
+
+    w_copies[0].wait()
+    w_copies[1].wait()
+
+    def pair_sums(j):
+        lhs = jnp.concatenate([spikes[gateup_ref[j, t * kk + k]] for k in range(kk)], axis=1)
+        rhs = jnp.concatenate([gate[j], up[j]], axis=1)
+        return jnp.dot(lhs, rhs, preferred_element_type=F32)
+
+    def gu_copy(i):
+        return send(snd_gu.at[i], rcv_gu.at[i], gu_s.at[i], gu_r.at[i], dev_y)
+
+    def rate_copy(i):
+        j = t * mine + i
+        return send(rate.at[j], rate.at[j], rt_s.at[i], rt_r.at[i], dev_y)
+
+    def give(i, carry):
+        snd_gu[i] = pair_sums((1 - t) * mine + i).astype(BF16)
+        gu_copy(i).start()
+        return carry
+
+    def take(i, carry):
+        j = t * mine + i
+        own = pair_sums(j)
+        gu_copy(i).wait_recv()
+        total = own + rcv_gu[i].astype(F32)
+        gate_sum = total[:, :128]
+        current = gate_sum / (1.0 + jnp.exp(-gate_sum)) * total[:, 128:]
+        limit = jnp.exp2(hid_exp_ref[pl.ds(j, 1), :].astype(F32)).astype(BF16).astype(F32)
+        rate[j] = jnp.minimum(jnp.maximum(current, -limit), limit).astype(BF16)
+        rate_copy(i).start()
+        return carry
+
+    lax.fori_loop(0, mine, give, 0)
+    lax.fori_loop(0, mine, take, 0)
+    w_copies[2].wait()
+    for i in range(mine):
+        rate_copy(i).wait_recv()
+
+    def down_chunk(g):
+        lhs = jnp.concatenate([rate[j] for j in range(columns)], axis=1)
+        cols = []
+        for h in range(parts):
+            n = g * parts + h
+            cols.append(
+                jnp.concatenate([down[j, slot_of_ref[j, n]] for j in range(columns)], axis=0)
+            )
+        return jnp.dot(lhs, jnp.concatenate(cols, axis=1), preferred_element_type=F32)
+
+    def core_copy(i):
+        return send(snd_c.at[i], rcv_c.at[i], c_s.at[i], c_r.at[i], dev_c)
+
+    def x_copy(i):
+        return send(snd_x.at[i], rcv_x.at[i], x_s.at[i], x_r.at[i], dev_x)
+
+    def y_copy(i):
+        return send(snd_y.at[i], rcv_y.at[i], y_s.at[i], y_r.at[i], dev_y)
+
+    def give_core_far(i, carry):
+        snd_c[i] = down_chunk(chunk(i, 1 - x, 1 - c)).astype(BF16)
+        core_copy(i).start()
+        return carry
+
+    def give_core_near(i, carry):
+        snd_c[4 + i] = down_chunk(chunk(i, x, 1 - c)).astype(BF16)
+        core_copy(4 + i).start()
+        return carry
+
+    def give_x(i, carry):
+        own = down_chunk(chunk(i, 1 - x, c))
+        core_copy(i).wait_recv()
+        snd_x[i] = (own + rcv_c[i].astype(F32)).astype(BF16)
+        x_copy(i).start()
+        return carry
+
+    def keep(i, carry):
+        own = down_chunk(chunk(i, x, c))
+        core_copy(4 + i).wait_recv()
+        acc[i] = own + rcv_c[4 + i].astype(F32)
+        return carry
+
+    my_rows = pl.ds(pl.multiple_of(t * half, half), half)
+    peer_rows = pl.ds(pl.multiple_of((1 - t) * half, half), half)
+
+    def give_y(i, carry):
+        x_copy(i).wait_recv()
+        snd_y[i] = (acc[i, peer_rows, :] + rcv_x[i, peer_rows, :].astype(F32)).astype(BF16)
+        y_copy(i).start()
+        return carry
+
+    lax.fori_loop(0, 4, give_core_far, 0)
+    lax.fori_loop(0, 4, give_x, 0)
+    lax.fori_loop(0, 4, give_core_near, 0)
+    lax.fori_loop(0, 4, keep, 0)
+    lax.fori_loop(0, 4, give_y, 0)
+
+    def own_sum(i):
+        y_copy(i).wait_recv()
+        return (
+            acc[i, my_rows, :] + rcv_x[i, my_rows, :].astype(F32) + rcv_y[i].astype(F32)
+        )
+
+    zs = []
+    for d in (2, 1, 3):
+        snd_z[d - 1] = own_sum(z_at(d)).astype(BF16)
+        zs.append(
+            start(send(snd_z.at[d - 1], rcv_z.at[d - 1], z_s.at[d - 1], z_r.at[d - 1], dev_z(d)))
+        )
+    total = own_sum(z)
+    for copy, d in zip(zs, (2, 1, 3)):
+        copy.wait_recv()
+        total = total + rcv_z[d - 1].astype(F32)
+    final[my_rows, :] = total.astype(BF16)
+    fin = start(send(final.at[my_rows], final.at[my_rows], fin_s.at[0], fin_r.at[0], dev_y))
+    slot_rows = lax.broadcasted_iota(jnp.int32, (slots, live), 0) + t * slots
+    live_lanes = lax.broadcasted_iota(jnp.int32, (slots, live), 1)
+    place = jnp.where(slot_target(lengths, slot_rows, side) == live_lanes, 1.0, 0.0).astype(BF16)
+    fin.wait_recv()
+    out_ref[...] = jnp.dot(place, final[...], preferred_element_type=F32).astype(BF16)
+
+    for copy in sent:
+        copy.wait_send()
+    for i in range(mine):
+        gu_copy(i).wait_send()
+        rate_copy(i).wait_send()
+    for i in range(8):
+        core_copy(i).wait_send()
+    for i in range(4):
+        x_copy(i).wait_send()
+        y_copy(i).wait_send()
+
+
+def sign_matrix(size):
+    index = np.arange(size)
+    shared = index[:, None] & index[None, :]
+    parity = np.zeros_like(shared)
+    for bit_number in range(max(1, (size - 1).bit_length())):
+        parity ^= (shared >> bit_number) & 1
+    return 1 - 2 * parity
+
+
+def local_kernel(
+    tokens,
+    seq_lengths,
+    in_exponents,
+    hidden_exponents,
+    gateup_blocks,
+    down_blocks,
+    gate_values,
+    up_values,
+    down_values,
+):
+    slots, width = tokens.shape
+    columns, kk, side, _ = gate_values.shape
+    model_width = in_exponents.shape[0]
+    blocks = model_width // side
+    chunks = model_width // width
+    mine = columns // 2
+    half = slots // 2
+    t = lax.axis_index("tok")
+    held = lax.dynamic_slice_in_dim(down_blocks, t * kk, kk, axis=1)
+    match = held[:, :, None] == jnp.arange(blocks, dtype=jnp.int32)[None, None, :]
+    number = jnp.arange(1, kk + 1, dtype=jnp.int32)[None, :, None]
+    slot_of = jnp.sum(jnp.where(match, number, 0), axis=1)
+
+    vmem = pl.BlockSpec(memory_space=pltpu.VMEM)
+    smem = pl.BlockSpec(memory_space=pltpu.SMEM)
+    anywhere = pl.BlockSpec(memory_space=pl.ANY)
+    dma = lambda n: pltpu.SemaphoreType.DMA((n,))
+    buf = lambda *shape: pltpu.VMEM(shape, BF16)
+    return pl.pallas_call(
+        body,
+        out_shape=jax.ShapeDtypeStruct((slots, width), BF16),
+        in_specs=[smem] * 3 + [vmem] * 4 + [anywhere] * 3,
+        out_specs=vmem,
+        scratch_shapes=[
+            buf(columns, kk * side, side),
+            buf(columns, kk * side, side),
+            buf(columns, kk + 1, side, side),
+            buf(slots, width),
+            buf(chunks, slots, width),
+            pltpu.VMEM((chunks, slots, width), F32),
+            pltpu.VMEM((blocks, side), F32),
+            buf(blocks, slots, side),
+            buf(mine, slots, 2 * side),
+            buf(mine, slots, 2 * side),
+            buf(columns, slots, side),
+            buf(8, slots, width),
+            buf(8, slots, width),
+            buf(4, slots, width),
+            buf(4, slots, width),
+            pltpu.VMEM((4, slots, width), F32),
+            buf(4, half, width),
+            buf(4, half, width),
+            buf(3, half, width),
+            buf(3, half, width),
+            buf(slots, width),
+            dma(3),
+            dma(1),
+            dma(1),
+            dma(3),
+            dma(3),
+            dma(4),
+            dma(4),
+            dma(8),
+            dma(8),
+            dma(mine),
+            dma(mine),
+            dma(mine),
+            dma(mine),
+            dma(8),
+            dma(8),
+            dma(4),
+            dma(4),
+            dma(4),
+            dma(4),
+            dma(3),
+            dma(3),
+            dma(1),
+            dma(1),
+        ],
+        compiler_params=pltpu.CompilerParams(
+            collective_id=0, has_side_effects=True, vmem_limit_bytes=40 * 1024 * 1024
+        ),
+        name="spiking_ffn",
+    )(
+        seq_lengths,
+        gateup_blocks,
+        slot_of,
+        tokens,
+        in_exponents.reshape(blocks, side),
+        hidden_exponents.reshape(columns, side),
+        jnp.asarray(sign_matrix(width), BF16),
+        gate_values.reshape(columns, kk * side, side),
+        up_values.reshape(columns, kk * side, side),
+        down_values,
+    )
 
 
 def partner_2(value, axis, stride):
@@ -24,7 +473,7 @@
     return (1 - 2 * parity).astype(value_type)
 
 
-def local(
+def local_general(
     tokens,
     seq_lengths,
     in_exponents,
@@ -39,7 +488,9 @@
     model_width = in_exponents.shape[0]
     seq_width = slot_count // SEQS_DEV
     tok_index = lax.axis_index("tok")
-    seq_ends = jnp.cumsum(seq_lengths)
+    seq_count = seq_lengths.shape[0]
+    earlier = jnp.tril(jnp.ones((seq_count, seq_count), jnp.int32))
+    seq_ends = jnp.sum(earlier * seq_lengths[None, :], axis=1)
     seq_starts = seq_ends - seq_lengths
     seq_ids = jnp.arange(seq_lengths.shape[0], dtype=jnp.int32)
     slot_ids = jnp.arange(slot_count, dtype=jnp.int32)
@@ -54,7 +505,10 @@
     owner_seq = jnp.sum((seq_ends[None, :] <= wanted[:, None]).astype(jnp.int32), axis=1)
     owner_match = owner_seq[:, None] == seq_ids[None, :]
     offset = wanted - jnp.sum(jnp.where(owner_match, seq_starts[None, :], 0), axis=1)
-    picked = jnp.take(pooled, owner_seq * seq_width + offset, axis=0)
+    picked_slot = owner_seq * seq_width + offset
+    pooled_slots = jnp.arange(pooled.shape[0], dtype=jnp.int32)
+    picker = (picked_slot[:, None] == pooled_slots[None, :]).astype(jnp.bfloat16)
+    picked = jnp.dot(picker, pooled, preferred_element_type=jnp.float32).astype(jnp.bfloat16)
     row_count = picked.shape[0]
     rotation_scale = 1.0 / math.sqrt(model_width)
     mixed_part = jnp.dot(
@@ -78,26 +532,20 @@
     block_size = gate_values.shape[2]
     block_count = model_width // block_size
     hidden_local = hidden_exponents.shape[0]
-    v_in = jnp.zeros((row_count, model_width), jnp.float32)
-    v_hidden = jnp.zeros((row_count, hidden_local), jnp.float32)
-    spike_count_sum = jnp.zeros((row_count, hidden_local), jnp.float32)
-    for step_index in range(TIME_STEPS):
-        v_in = v_in + rotated.astype(jnp.float32)
-        spike_in = jnp.clip(v_in, -in_limit, in_limit).astype(jnp.bfloat16)
-        v_in = v_in - spike_in.astype(jnp.float32)
-        chosen = jnp.take(
-            spike_in.reshape(row_count, block_count, block_size), gateup_blocks, axis=1
+    spike_in = jnp.clip(rotated.astype(jnp.float32), -in_limit, in_limit).astype(jnp.bfloat16)
+    block_ids = jnp.arange(block_count, dtype=jnp.int32)
+    gateup_place = (gateup_blocks[:, :, None] == block_ids[None, None, :]).astype(jnp.bfloat16)
+
+    def dense(values):
+        wide = jnp.einsum(
+            "hkbc,hkn->nbhc", values, gateup_place, preferred_element_type=jnp.float32
         )
-        gate_sum = jnp.einsum(
-            "rhkb,hkbc->rhc", chosen, gate_full, preferred_element_type=jnp.float32
-        )
-        upward = jnp.einsum("rhkb,hkbc->rhc", chosen, up_full, preferred_element_type=jnp.float32)
-        current = (jax.nn.silu(gate_sum) * upward).reshape(row_count, hidden_local)
-        v_hidden = v_hidden + current
-        spike_hidden = jnp.clip(v_hidden, -hidden_limit, hidden_limit)
-        v_hidden = v_hidden - spike_hidden
-        spike_count_sum = spike_count_sum + spike_hidden
-    spiking_rate = (spike_count_sum / TIME_STEPS).astype(jnp.bfloat16)
+        return wide.astype(jnp.bfloat16).reshape(model_width, hidden_local)
+
+    gate_sum = jnp.dot(spike_in, dense(gate_full), preferred_element_type=jnp.float32)
+    upward = jnp.dot(spike_in, dense(up_full), preferred_element_type=jnp.float32)
+    current = jax.nn.silu(gate_sum) * upward
+    spiking_rate = jnp.clip(current, -hidden_limit, hidden_limit).astype(jnp.bfloat16)
     indicator = (
         down_blocks[:, :, None] == jnp.arange(block_count, dtype=jnp.int32)[None, None, :]
     ).astype(jnp.bfloat16)
@@ -111,8 +559,11 @@
     summed = lax.psum_scatter(partial_block_value, "feat", scatter_dimension=1, tiled=True)
     returned = lax.all_gather(summed.astype(jnp.bfloat16), "tok", axis=0, tiled=True)
     source_row = jnp.where(live_slot, start_of + position, 0)
-    result_rows = jnp.take(returned, source_row, axis=0)
-    return jnp.where(live_slot[:, None], result_rows, jnp.zeros_like(result_rows))
+    returned_rows = jnp.arange(returned.shape[0], dtype=jnp.int32)
+    placer = (source_row[:, None] == returned_rows[None, :]) & live_slot[:, None]
+    return jnp.dot(
+        placer.astype(jnp.bfloat16), returned, preferred_element_type=jnp.float32
+    ).astype(jnp.bfloat16)
 
 
 def solution(mesh):
@@ -128,4 +579,6 @@
         P("feat", "tok", None, None),
     )
     out_specs = P("tok", "feat")
+    same_groups = dict(mesh.shape) == {"tok": 2, "feat": 16}
+    local = local_kernel if same_groups else local_general
     return jax.shard_map(local, mesh=mesh, in_specs=in_specs, out_specs=out_specs, check_vma=False)

time: 265 us -> 63.4 us (0.24)
  waiting for transfers between devices: 166 us -> 0 us
  Pallas kernels: 0 us -> 52.2 us
  blocking collectives: 34.6 us -> 0 us
  matrix products: 23.1 us -> 0 us
  between operations: 13.3 us -> 0.03 us
  starting transfers between devices: 6.99 us -> 0 us
  local copies, waits for them, and re-layouts: 16.5 us -> 10.6 us
  other arithmetic: 3.82 us -> 0.09 us
    all_gather x3 -> x0, waiting for transfers between devices: 100 us -> none  [the longest x1 50 us: local(): lax.all_gather(up_values, 'tok', axis=1, tiled=True)]
    reduce_scatter x1 -> x0, waiting for transfers between devices: 57.4 us -> none  [local(): lax.psum_scatter(partial_block_value, 'feat', scatter_dimension=1, tiled=...]
    pallas_call x0 -> x1, Pallas kernels: none -> 52.2 us  [local_kernel(): pl.pallas_call(body, out_shape=jax.ShapeDtypeStruct((slots, width), BF16)...]
    all_gather x3 -> x0, blocking collectives: 34.6 us -> none  [the longest x1 24.2 us: local(): lax.all_gather((mixed_part * rotation_scale).astype(jnp.bfloat16), 'feat'...]
    dot_general x11 -> x0, matrix products: 23.1 us -> none  [the longest x4 7.15 us: local(): jnp.einsum('rhkb,hkbc->rhc', chosen, up_full, preferred_element_type=jnp....]
    gather x6 -> x0, local copies, waits for them, and re-layouts: 8.9 us -> none  [the longest x4 7.35 us: local(): jnp.take(spike_in.reshape(row_count, block_count, block_size), gateup_blo...]
    ppermute x4 -> x0, waiting for transfers between devices: 7.52 us -> none  [partner_2(): return lax.ppermute(value, axis, pairs)]
    ppermute x4 -> x0, starting transfers between devices: 6.87 us -> none  [partner_2(): return lax.ppermute(value, axis, pairs)]
  transfers between devices with their start and end apart: 8 -> 0, of which waited for: 6 -> 0; matrix products, arithmetic and copies ran while one was open for 11% -> 0% of each run, Pallas kernels for 0% -> 0%
where the time goes in v1:
time: 63.4 us; the launch traced here: 63 us
  Pallas kernels  52.2 us (82%)
  local copies, waits for them, and re-layouts  10.6 us (17%)
    pallas_call x1, Pallas kernels, local_kernel(): pl.pallas_call(body, out_shape=jax.ShapeDtypeStruct((slots, width), BF16)...  52.2 us
    unnamed x21, local copies, waits for them, and re-layouts  10.6 us

profile of v1, /device:TPU:0, one launch (start us, length us, event | category | flops | bytes accessed | tf_op | source)
XLA Modules:
  0.0 63.0 jit_solution(7212385698818204114)
XLA Ops:
  0.0 0.0 copy-start
  0.0 0.7 %copy-done = s32[8,16]{1,0:T(8,128)S(1)} copy-done((s32[8,16]{1,0:T(8,128)S(1)}, s32[8,16]{1,0:T(8,128)}, u32[]{:S(2)}) %copy-start) | copy-done | bytes 536
  0.7 0.1 constant_dynamic-slice_fusion
  0.8 0.1 select_reduce_fusion.slot_of_ref
  0.9 0.0 copy-start.1
  0.9 1.6 %copy-done.1 = bf16[8,8,128,128]{3,2,1,0:T(8,128)(2,1)S(1)} copy-done((bf16[8,8,128,128]{3,2,1,0:T(8,128)(2,1)S(1)}, bf16[8,8,128,128]{3,2,1,0:T(8,128)(2,1)}, u32[]{:S(2)}) %copy-start.1) | copy-done | bytes 2097176
  2.5 0.0 copy-start.2
  2.5 1.6 %copy-done.2 = bf16[8,8,128,128]{3,2,1,0:T(8,128)(2,1)S(1)} copy-done((bf16[8,8,128,128]{3,2,1,0:T(8,128)(2,1)S(1)}, bf16[8,8,128,128]{3,2,1,0:T(8,128)(2,1)}, u32[]{:S(2)}) %copy-start.2) | copy-done | bytes 2097176
  4.0 0.0 copy-start.3
  4.0 1.6 %copy-done.3 = bf16[8,8,128,128]{3,2,1,0:T(8,128)(2,1)S(1)} copy-done((bf16[8,8,128,128]{3,2,1,0:T(8,128)(2,1)S(1)}, bf16[8,8,128,128]{3,2,1,0:T(8,128)(2,1)}, u32[]{:S(2)}) %copy-start.3) | copy-done | bytes 2097176
  5.6 0.0 copy-start.4
  5.6 0.9 %copy-done.4 = bf16[256,256]{1,0:T(8,128)(2,1)S(1)} copy-done((bf16[256,256]{1,0:T(8,128)(2,1)S(1)}, bf16[256,256]{1,0:T(8,128)(2,1)}, u32[]{:S(2)}) %copy-start.4) | copy-done | bytes 131096
  6.5 0.0 copy-start.5
  6.5 0.8 %copy-done.5 = bf16[128,256]{1,0:T(8,128)(2,1)S(1)} copy-done((bf16[128,256]{1,0:T(8,128)(2,1)S(1)}, bf16[128,256]{1,0:T(8,128)(2,1)}, u32[]{:S(2)}) %copy-start.5) | copy-done | bytes 65560
  7.4 0.0 copy-start.6
  7.4 0.7 %copy-done.6 = s32[4096]{0:T(1024)S(1)} copy-done((s32[4096]{0:T(1024)S(1)}, s32[4096]{0:T(1024)}, u32[]{:S(2)}) %copy-start.6) | copy-done | bytes 16408
  8.1 0.0 copy-start.7
  8.1 0.7 %copy-done.7 = s32[8,16]{1,0:T(8,128)S(1)} copy-done((s32[8,16]{1,0:T(8,128)S(1)}, s32[8,16]{1,0:T(8,128)}, u32[]{:S(2)}) %copy-start.7) | copy-done | bytes 536
  8.8 0.0 copy-start.8
  8.8 0.7 %copy-done.8 = s32[1024]{0:T(1024)S(1)} copy-done((s32[1024]{0:T(1024)S(1)}, s32[1024]{0:T(1024)}, u32[]{:S(2)}) %copy-start.8) | copy-done | bytes 4120
  9.5 0.0 copy-start.9
  9.5 0.7 %copy-done.9 = s32[4]{0:T(128)S(1)} copy-done((s32[4]{0:T(128)S(1)}, s32[4]{0:T(128)}, u32[]{:S(2)}) %copy-start.9) | copy-done | bytes 40
  10.1 52.2 %spiking_ffn.1 = bf16[128,256]{1,0:T(8,128)(2,1)S(1)} custom-call(s32[4]{0:T(128)S(1)} %copy-done.9, s32[8,16]{1,0:T(8,128)S(1)} %copy-done.7, s32[8,32]{1,0:T(8,128)S(1)} %select_reduce_fusion.slot_of_ref, bf16[128,256]{1,0:T(8,128)(2,1)S(1)} %copy-done.5, s32[32,128]{1,0:T(8,128)S(1)} %bitcast.6, s32[8,128]{1,0:T(8,128)S(1)} %bitcast.7, ...), custom_call_target="tpu_custom_call" | custom-call | tf_op jit(solution)/shard_map/spiking_ffn/pallas_call | solution.py:392
  62.4 0.6 %copy.12 = bf16[128,256]{1,0:T(8,128)(2,1)} copy(bf16[128,256]{1,0:T(8,128)(2,1)S(1)} %spiking_ffn.1) | data formatting | bytes 131072
  (1 shorter events, 0.0 us)
Async XLA Ops:
  0.0 0.7 %copy-start = (s32[8,16]{1,0:T(8,128)S(1)}, s32[8,16]{1,0:T(8,128)}, u32[]{:S(2)}) copy-start(s32[8,16]{1,0:T(8,128)} %param.15) | copy-start | bytes 1540
  0.9 1.6 %copy-start.1 = (bf16[8,8,128,128]{3,2,1,0:T(8,128)(2,1)S(1)}, bf16[8,8,128,128]{3,2,1,0:T(8,128)(2,1)}, u32[]{:S(2)}) copy-start(bf16[8,8,128,128]{3,2,1,0:T(8,128)(2,1)} %param.16) | copy-start | bytes 6291460
  2.5 1.6 %copy-start.2 = (bf16[8,8,128,128]{3,2,1,0:T(8,128)(2,1)S(1)}, bf16[8,8,128,128]{3,2,1,0:T(8,128)(2,1)}, u32[]{:S(2)}) copy-start(bf16[8,8,128,128]{3,2,1,0:T(8,128)(2,1)} %param.17) | copy-start | bytes 6291460
  4.0 1.6 %copy-start.3 = (bf16[8,8,128,128]{3,2,1,0:T(8,128)(2,1)S(1)}, bf16[8,8,128,128]{3,2,1,0:T(8,128)(2,1)}, u32[]{:S(2)}) copy-start(bf16[8,8,128,128]{3,2,1,0:T(8,128)(2,1)} %down_hbm.1) | copy-start | bytes 6291460
  5.6 0.9 %copy-start.4 = (bf16[256,256]{1,0:T(8,128)(2,1)S(1)}, bf16[256,256]{1,0:T(8,128)(2,1)}, u32[]{:S(2)}) copy-start(bf16[256,256]{1,0:T(8,128)(2,1)} %constant.16.clone.sign_ref) | copy-start | bytes 393220
  6.5 0.8 %copy-start.5 = (bf16[128,256]{1,0:T(8,128)(2,1)S(1)}, bf16[128,256]{1,0:T(8,128)(2,1)}, u32[]{:S(2)}) copy-start(bf16[128,256]{1,0:T(8,128)(2,1)} %tok_ref.1) | copy-start | bytes 196612
  7.4 0.7 %copy-start.6 = (s32[4096]{0:T(1024)S(1)}, s32[4096]{0:T(1024)}, u32[]{:S(2)}) copy-start(s32[4096]{0:T(1024)} %param.12) | copy-start | bytes 49156
  8.1 0.7 %copy-start.7 = (s32[8,16]{1,0:T(8,128)S(1)}, s32[8,16]{1,0:T(8,128)}, u32[]{:S(2)}) copy-start(s32[8,16]{1,0:T(8,128)} %gateup_ref.1) | copy-start | bytes 1540
  8.8 0.7 %copy-start.8 = (s32[1024]{0:T(1024)S(1)}, s32[1024]{0:T(1024)}, u32[]{:S(2)}) copy-start(s32[1024]{0:T(1024)} %param.13) | copy-start | bytes 12292
  9.5 0.7 %copy-start.9 = (s32[4]{0:T(128)S(1)}, s32[4]{0:T(128)}, u32[]{:S(2)}) copy-start(s32[4]{0:T(128)} %lengths_ref.1) | copy-start | bytes 52

commit v2 on v1

--- a/solution.py
+++ b/solution.py
@@ -2,7 +2,6 @@
 
 import jax
 import jax.numpy as jnp
-import numpy as np
 from jax import lax
 from jax.experimental import pallas as pl
 from jax.experimental.pallas import tpu as pltpu
@@ -29,17 +28,18 @@
 
 
 def body(
-    lengths_ref,
-    gateup_ref,
-    slot_of_ref,
+    table_ref,
+    tok_hbm,
+    in_exp_hbm,
+    hid_exp_hbm,
+    gate_hbm,
+    up_hbm,
+    down_hbm,
+    out_ref,
     tok_ref,
     in_exp_ref,
     hid_exp_ref,
     sign_ref,
-    gate_hbm,
-    up_hbm,
-    down_hbm,
-    out_ref,
     gate,
     up,
     down,
@@ -96,7 +96,9 @@
     side = slots // SEQS_DEV
     columns = rate.shape[0]
     mine = columns // 2
-    kk = gateup_ref.shape[1] // 2
+    kk = down.shape[1] - 1
+    blocks = in_limit.shape[0]
+    seq_at = blocks + kk
 
     dev_y = (1 - t, f)
     dev_c = (t, f + 1 - 2 * c)
@@ -121,6 +123,14 @@
             device_id_type=MESH_ID,
         )
 
+    tok_copy = pltpu.make_async_copy(tok_hbm, tok_ref, w_sem.at[3])
+    exp_copies = [
+        pltpu.make_async_copy(in_exp_hbm, in_exp_ref, w_sem.at[4]),
+        pltpu.make_async_copy(hid_exp_hbm, hid_exp_ref, w_sem.at[5]),
+    ]
+    tok_copy.start()
+    for copy in exp_copies:
+        copy.start()
     w_copies = [
         pltpu.make_async_copy(gate_hbm, gate, w_sem.at[0]),
         pltpu.make_async_copy(up_hbm, up, w_sem.at[1]),
@@ -135,11 +145,22 @@
         pl.semaphore_signal(barrier, inc=1, device_id=dev, device_id_type=MESH_ID)
     pl.semaphore_wait(barrier, len(partners))
 
+    tok_copy.wait()
+
     raw = send(tok_ref, peer_tok, raw_s.at[0], raw_r.at[0], dev_y)
     raw.start()
     down[:, pl.ds(0, 1)] = jnp.zeros((columns, 1) + down.shape[2:], BF16)
+    index = lax.broadcasted_iota(jnp.int32, (width, width), 0)
+    parity = index & lax.broadcasted_iota(jnp.int32, (width, width), 1)
+    shift = 1
+    while shift < width.bit_length():
+        parity = parity ^ (parity >> shift)
+        shift *= 2
+    sign_ref[...] = (1 - 2 * (parity & 1)).astype(F32).astype(BF16)
+    for copy in exp_copies:
+        copy.wait()
     in_limit[...] = jnp.exp2(in_exp_ref[...].astype(F32)).astype(BF16).astype(F32)
-    lengths = [lengths_ref[q] for q in range(lengths_ref.shape[0])]
+    lengths = [table_ref[0, seq_at + q] for q in range(table_ref.shape[1] - seq_at)]
     rows = lax.broadcasted_iota(jnp.int32, (live, slots), 0)
     lane_slots = lax.broadcasted_iota(jnp.int32, (live, slots), 1)
 
@@ -224,7 +245,7 @@
     w_copies[1].wait()
 
     def pair_sums(j):
-        lhs = jnp.concatenate([spikes[gateup_ref[j, t * kk + k]] for k in range(kk)], axis=1)
+        lhs = jnp.concatenate([spikes[table_ref[j, blocks + k]] for k in range(kk)], axis=1)
         rhs = jnp.concatenate([gate[j], up[j]], axis=1)
         return jnp.dot(lhs, rhs, preferred_element_type=F32)
 
@@ -264,10 +285,13 @@
         for h in range(parts):
             n = g * parts + h
             cols.append(
-                jnp.concatenate([down[j, slot_of_ref[j, n]] for j in range(columns)], axis=0)
+                jnp.concatenate([down[j, table_ref[j, n]] for j in range(columns)], axis=0)
             )
         return jnp.dot(lhs, jnp.concatenate(cols, axis=1), preferred_element_type=F32)
 
+    def z_turn(i):
+        return z_at(jnp.where(i < 2, 2 + i, 3 - i))
+
     def core_copy(i):
         return send(snd_c.at[i], rcv_c.at[i], c_s.at[i], c_r.at[i], dev_c)
 
@@ -278,24 +302,24 @@
         return send(snd_y.at[i], rcv_y.at[i], y_s.at[i], y_r.at[i], dev_y)
 
     def give_core_far(i, carry):
-        snd_c[i] = down_chunk(chunk(i, 1 - x, 1 - c)).astype(BF16)
+        snd_c[i] = down_chunk(chunk(z_turn(i), 1 - x, 1 - c)).astype(BF16)
         core_copy(i).start()
         return carry
 
     def give_core_near(i, carry):
-        snd_c[4 + i] = down_chunk(chunk(i, x, 1 - c)).astype(BF16)
+        snd_c[4 + i] = down_chunk(chunk(z_turn(i), x, 1 - c)).astype(BF16)
         core_copy(4 + i).start()
         return carry
 
     def give_x(i, carry):
-        own = down_chunk(chunk(i, 1 - x, c))
+        own = down_chunk(chunk(z_turn(i), 1 - x, c))
         core_copy(i).wait_recv()
         snd_x[i] = (own + rcv_c[i].astype(F32)).astype(BF16)
         x_copy(i).start()
         return carry
 
     def keep(i, carry):
-        own = down_chunk(chunk(i, x, c))
+        own = down_chunk(chunk(z_turn(i), x, c))
         core_copy(4 + i).wait_recv()
         acc[i] = own + rcv_c[4 + i].astype(F32)
         return carry
@@ -322,13 +346,13 @@
         )
 
     zs = []
-    for d in (2, 1, 3):
-        snd_z[d - 1] = own_sum(z_at(d)).astype(BF16)
+    for i, d in enumerate((2, 3, 1)):
+        snd_z[d - 1] = own_sum(i).astype(BF16)
         zs.append(
             start(send(snd_z.at[d - 1], rcv_z.at[d - 1], z_s.at[d - 1], z_r.at[d - 1], dev_z(d)))
         )
-    total = own_sum(z)
-    for copy, d in zip(zs, (2, 1, 3)):
+    total = own_sum(3)
+    for copy, d in zip(zs, (2, 3, 1)):
         copy.wait_recv()
         total = total + rcv_z[d - 1].astype(F32)
     final[my_rows, :] = total.astype(BF16)
@@ -349,15 +373,6 @@
     for i in range(4):
         x_copy(i).wait_send()
         y_copy(i).wait_send()
-
-
-def sign_matrix(size):
-    index = np.arange(size)
-    shared = index[:, None] & index[None, :]
-    parity = np.zeros_like(shared)
-    for bit_number in range(max(1, (size - 1).bit_length())):
-        parity ^= (shared >> bit_number) & 1
-    return 1 - 2 * parity
 
 
 def local_kernel(
@@ -384,6 +399,16 @@
     number = jnp.arange(1, kk + 1, dtype=jnp.int32)[None, :, None]
     slot_of = jnp.sum(jnp.where(match, number, 0), axis=1)
 
+    seq_count = seq_lengths.shape[0]
+    table = jnp.concatenate(
+        [
+            slot_of,
+            lax.dynamic_slice_in_dim(gateup_blocks, t * kk, kk, axis=1),
+            jnp.broadcast_to(seq_lengths[None, :], (columns, seq_count)),
+        ],
+        axis=1,
+    )
+
     vmem = pl.BlockSpec(memory_space=pltpu.VMEM)
     smem = pl.BlockSpec(memory_space=pltpu.SMEM)
     anywhere = pl.BlockSpec(memory_space=pl.ANY)
@@ -392,9 +417,13 @@
     return pl.pallas_call(
         body,
         out_shape=jax.ShapeDtypeStruct((slots, width), BF16),
-        in_specs=[smem] * 3 + [vmem] * 4 + [anywhere] * 3,
+        in_specs=[smem] + [anywhere] * 6,
         out_specs=vmem,
         scratch_shapes=[
+            buf(slots, width),
+            pltpu.VMEM((blocks, side), jnp.int32),
+            pltpu.VMEM((columns, side), jnp.int32),
+            buf(width, width),
             buf(columns, kk * side, side),
             buf(columns, kk * side, side),
             buf(columns, kk + 1, side, side),
@@ -416,7 +445,7 @@
             buf(3, half, width),
             buf(3, half, width),
             buf(slots, width),
-            dma(3),
+            dma(6),
             dma(1),
             dma(1),
             dma(3),
@@ -441,17 +470,14 @@
             dma(1),
         ],
         compiler_params=pltpu.CompilerParams(
-            collective_id=0, has_side_effects=True, vmem_limit_bytes=40 * 1024 * 1024
+            collective_id=0, has_side_effects=True, vmem_limit_bytes=60 * 1024 * 1024
         ),
         name="spiking_ffn",
     )(
-        seq_lengths,
-        gateup_blocks,
-        slot_of,
+        table,
         tokens,
         in_exponents.reshape(blocks, side),
         hidden_exponents.reshape(columns, side),
-        jnp.asarray(sign_matrix(width), BF16),
         gate_values.reshape(columns, kk * side, side),
         up_values.reshape(columns, kk * side, side),
         down_values,

time: 63.4 us -> 56.7 us (0.89)
  local copies, waits for them, and re-layouts: 10.6 us -> 2.98 us
  other arithmetic: 0.09 us -> 0.76 us
    unnamed x21 -> x1, local copies, waits for them, and re-layouts: 10.6 us -> 1.47 us
    concatenate x0 -> x1, local copies, waits for them, and re-layouts: none -> 0.73 us  [local_kernel(): jnp.concatenate([slot_of, lax.dynamic_slice_in_dim(gateup_blocks, t * kk,...]
    dynamic_slice x1, local copies, waits for them, and re-layouts: 0.07 us -> 0.77 us  [local_kernel(): lax.dynamic_slice_in_dim(gateup_blocks, t * kk, kk, axis=1)]
    concatenate x0 -> x1, other arithmetic: none -> 0.67 us  [local_kernel(): jnp.concatenate([slot_of, lax.dynamic_slice_in_dim(gateup_blocks, t * kk,...]
where the time goes in v2:
time: 56.7 us; the launch traced here: 56.4 us
  Pallas kernels  52.7 us (93%)
  local copies, waits for them, and re-layouts  2.98 us (5%)
  other arithmetic  0.76 us (1%)
    pallas_call x1, Pallas kernels, local_kernel(): pl.pallas_call(body, out_shape=jax.ShapeDtypeStruct((slots, width), BF16)...  52.7 us
    unnamed x1, local copies, waits for them, and re-layouts  1.47 us

profile of v2, /device:TPU:0, one launch (start us, length us, event | category | flops | bytes accessed | tf_op | source)
XLA Modules:
  0.0 56.4 jit_solution(12143544506539117383)
XLA Ops:
  0.0 0.7 %pad.2.clone = s32[44]{0:T(128)S(1)} pad(s32[4]{0:T(128)} %param.10, s32[]{:T(128)} %constant.2.clone.1), padding=40_0 | pad | bytes 196 | tf_op jit(solution)/shard_map/concatenate | solution.py:403
  0.7 0.8 %constant_dynamic-slice_fusion = (s32[8,8]{1,0:T(8,128)S(1)}, s32[8,8]{1,0:T(8,128)S(1)}) fusion(s32[8,16]{1,0:T(8,128)} %param.13, s32[]{:T(128)S(6)} %select_n.8, s32[8,16]{1,0:T(8,128)} %param.14), kind=kLoop, calls=%fused_computation.4 | loop fusion | bytes 1028 | tf_op jit(solution)/shard_map/dynamic_slice | solution.py:406
  1.5 0.1 select_reduce_fusion
  1.6 0.7 %add_add_fusion.table_ref = s32[8,44]{1,0:T(8,128)} fusion(s32[8,8]{1,0:T(8,128)S(1)} %get-tuple-element.5, s32[8,32]{1,0:T(8,128)S(1)} %select_reduce_fusion, s32[44]{0:T(128)S(1)} %pad.2.clone), kind=kLoop, calls=%fused_computation.2 | loop fusion | flops 704 | bytes 2864 | tf_op jit(solution)/shard_map/concatenate | solution.py:403
  2.3 52.7 %spiking_ffn.1 = bf16[128,256]{1,0:T(8,128)(2,1)} custom-call(s32[8,44]{1,0:T(8,128)} %add_add_fusion.table_ref, bf16[128,256]{1,0:T(8,128)(2,1)} %tok_hbm.1, s32[32,128]{1,0:T(8,128)} %bitcast.6, s32[8,128]{1,0:T(8,128)} %bitcast.7, bf16[8,1024,128]{2,1,0:T(8,128)(2,1)} %bitcast.4, bf16[8,1024,128]{2,1,0:T(8,128)(2,1)} %bitcast.5, ...), custom_call_target="tpu_custom_call" | custom-call | tf_op jit(solution)/shard_map/spiking_ffn/pallas_call | solution.py:417
  55.0 1.5 %copy.11 = bf16[128,256]{1,0:T(8,128)(2,1)} copy(bf16[128,256]{1,0:T(8,128)(2,1)} %spiking_ffn.1) | data formatting | bytes 131072
  (1 shorter events, 0.0 us)

commit v3 on v2

--- a/solution.py
+++ b/solution.py
@@ -28,7 +28,9 @@
 
 
 def body(
-    table_ref,
+    lengths_hbm,
+    gateup_hbm,
+    held_hbm,
     tok_hbm,
     in_exp_hbm,
     hid_exp_hbm,
@@ -36,6 +38,11 @@
     up_hbm,
     down_hbm,
     out_ref,
+    lengths_ref,
+    gateup_ref,
+    held_ref,
+    slot_vec,
+    slot_of_ref,
     tok_ref,
     in_exp_ref,
     hid_exp_ref,
@@ -60,7 +67,6 @@
     rcv_y,
     snd_z,
     rcv_z,
-    final,
     w_sem,
     raw_s,
     raw_r,
@@ -82,8 +88,6 @@
     y_r,
     z_s,
     z_r,
-    fin_s,
-    fin_r,
 ):
     t = lax.axis_index("tok")
     f = lax.axis_index("feat")
@@ -92,13 +96,10 @@
     c = f % 2
     slots, width = tok_ref.shape
     live = slots
-    half = live // 2
     side = slots // SEQS_DEV
     columns = rate.shape[0]
     mine = columns // 2
     kk = down.shape[1] - 1
-    blocks = in_limit.shape[0]
-    seq_at = blocks + kk
 
     dev_y = (1 - t, f)
     dev_c = (t, f + 1 - 2 * c)
@@ -127,6 +128,9 @@
     exp_copies = [
         pltpu.make_async_copy(in_exp_hbm, in_exp_ref, w_sem.at[4]),
         pltpu.make_async_copy(hid_exp_hbm, hid_exp_ref, w_sem.at[5]),
+        pltpu.make_async_copy(lengths_hbm, lengths_ref, w_sem.at[6]),
+        pltpu.make_async_copy(gateup_hbm, gateup_ref, w_sem.at[7]),
+        pltpu.make_async_copy(held_hbm, held_ref, w_sem.at[8]),
     ]
     tok_copy.start()
     for copy in exp_copies:
@@ -159,8 +163,16 @@
     sign_ref[...] = (1 - 2 * (parity & 1)).astype(F32).astype(BF16)
     for copy in exp_copies:
         copy.wait()
+    held = jnp.where(t == 0, held_ref[:, :kk], held_ref[:, kk:])
+    block_ids = lax.broadcasted_iota(jnp.int32, slot_vec.shape, 1)
+    slot_of = jnp.zeros(slot_vec.shape, jnp.int32)
+    for k in range(kk):
+        slot_of = jnp.where(held[:, k : k + 1] == block_ids, k + 1, slot_of)
+    slot_vec[...] = slot_of
+    slot_copy = pltpu.make_async_copy(slot_vec, slot_of_ref, w_sem.at[9])
+    slot_copy.start()
     in_limit[...] = jnp.exp2(in_exp_ref[...].astype(F32)).astype(BF16).astype(F32)
-    lengths = [table_ref[0, seq_at + q] for q in range(table_ref.shape[1] - seq_at)]
+    lengths = [lengths_ref[q] for q in range(lengths_ref.shape[0])]
     rows = lax.broadcasted_iota(jnp.int32, (live, slots), 0)
     lane_slots = lax.broadcasted_iota(jnp.int32, (live, slots), 1)
 
@@ -245,7 +257,7 @@
     w_copies[1].wait()
 
     def pair_sums(j):
-        lhs = jnp.concatenate([spikes[table_ref[j, blocks + k]] for k in range(kk)], axis=1)
+        lhs = jnp.concatenate([spikes[gateup_ref[j, t * kk + k]] for k in range(kk)], axis=1)
         rhs = jnp.concatenate([gate[j], up[j]], axis=1)
         return jnp.dot(lhs, rhs, preferred_element_type=F32)
 
@@ -276,6 +288,7 @@
     lax.fori_loop(0, mine, give, 0)
     lax.fori_loop(0, mine, take, 0)
     w_copies[2].wait()
+    slot_copy.wait()
     for i in range(mine):
         rate_copy(i).wait_recv()
 
@@ -285,7 +298,7 @@
         for h in range(parts):
             n = g * parts + h
             cols.append(
-                jnp.concatenate([down[j, table_ref[j, n]] for j in range(columns)], axis=0)
+                jnp.concatenate([down[j, slot_of_ref[j, n]] for j in range(columns)], axis=0)
             )
         return jnp.dot(lhs, jnp.concatenate(cols, axis=1), preferred_element_type=F32)
 
@@ -297,9 +310,6 @@
 
     def x_copy(i):
         return send(snd_x.at[i], rcv_x.at[i], x_s.at[i], x_r.at[i], dev_x)
-
-    def y_copy(i):
-        return send(snd_y.at[i], rcv_y.at[i], y_s.at[i], y_r.at[i], dev_y)
 
     def give_core_far(i, carry):
         snd_c[i] = down_chunk(chunk(z_turn(i), 1 - x, 1 - c)).astype(BF16)
@@ -324,26 +334,14 @@
         acc[i] = own + rcv_c[4 + i].astype(F32)
         return carry
 
-    my_rows = pl.ds(pl.multiple_of(t * half, half), half)
-    peer_rows = pl.ds(pl.multiple_of((1 - t) * half, half), half)
-
-    def give_y(i, carry):
-        x_copy(i).wait_recv()
-        snd_y[i] = (acc[i, peer_rows, :] + rcv_x[i, peer_rows, :].astype(F32)).astype(BF16)
-        y_copy(i).start()
-        return carry
-
     lax.fori_loop(0, 4, give_core_far, 0)
     lax.fori_loop(0, 4, give_x, 0)
     lax.fori_loop(0, 4, give_core_near, 0)
     lax.fori_loop(0, 4, keep, 0)
-    lax.fori_loop(0, 4, give_y, 0)
 
     def own_sum(i):
-        y_copy(i).wait_recv()
-        return (
-            acc[i, my_rows, :] + rcv_x[i, my_rows, :].astype(F32) + rcv_y[i].astype(F32)
-        )
+        x_copy(i).wait_recv()
+        return acc[i] + rcv_x[i].astype(F32)
 
     zs = []
     for i, d in enumerate((2, 3, 1)):
@@ -355,13 +353,14 @@
     for copy, d in zip(zs, (2, 3, 1)):
         copy.wait_recv()
         total = total + rcv_z[d - 1].astype(F32)
-    final[my_rows, :] = total.astype(BF16)
-    fin = start(send(final.at[my_rows], final.at[my_rows], fin_s.at[0], fin_r.at[0], dev_y))
+    snd_y[...] = total.astype(BF16)
+    fin = start(send(snd_y, rcv_y, y_s.at[0], y_r.at[0], dev_y))
     slot_rows = lax.broadcasted_iota(jnp.int32, (slots, live), 0) + t * slots
     live_lanes = lax.broadcasted_iota(jnp.int32, (slots, live), 1)
     place = jnp.where(slot_target(lengths, slot_rows, side) == live_lanes, 1.0, 0.0).astype(BF16)
     fin.wait_recv()
-    out_ref[...] = jnp.dot(place, final[...], preferred_element_type=F32).astype(BF16)
+    result = (total + rcv_y[...].astype(F32)).astype(BF16)
+    out_ref[...] = jnp.dot(place, result, preferred_element_type=F32).astype(BF16)
 
     for copy in sent:
         copy.wait_send()
@@ -372,7 +371,6 @@
         core_copy(i).wait_send()
     for i in range(4):
         x_copy(i).wait_send()
-        y_copy(i).wait_send()
 
 
 def local_kernel(
@@ -392,34 +390,22 @@
     blocks = model_width // side
     chunks = model_width // width
     mine = columns // 2
-    half = slots // 2
     t = lax.axis_index("tok")
-    held = lax.dynamic_slice_in_dim(down_blocks, t * kk, kk, axis=1)
-    match = held[:, :, None] == jnp.arange(blocks, dtype=jnp.int32)[None, None, :]
-    number = jnp.arange(1, kk + 1, dtype=jnp.int32)[None, :, None]
-    slot_of = jnp.sum(jnp.where(match, number, 0), axis=1)
-
-    seq_count = seq_lengths.shape[0]
-    table = jnp.concatenate(
-        [
-            slot_of,
-            lax.dynamic_slice_in_dim(gateup_blocks, t * kk, kk, axis=1),
-            jnp.broadcast_to(seq_lengths[None, :], (columns, seq_count)),
-        ],
-        axis=1,
-    )
-
     vmem = pl.BlockSpec(memory_space=pltpu.VMEM)
-    smem = pl.BlockSpec(memory_space=pltpu.SMEM)
     anywhere = pl.BlockSpec(memory_space=pl.ANY)
     dma = lambda n: pltpu.SemaphoreType.DMA((n,))
     buf = lambda *shape: pltpu.VMEM(shape, BF16)
     return pl.pallas_call(
         body,
         out_shape=jax.ShapeDtypeStruct((slots, width), BF16),
-        in_specs=[smem] + [anywhere] * 6,
+        in_specs=[anywhere] * 9,
         out_specs=vmem,
         scratch_shapes=[
+            pltpu.SMEM(seq_lengths.shape, jnp.int32),
+            pltpu.SMEM(gateup_blocks.shape, jnp.int32),
+            pltpu.VMEM(down_blocks.shape, jnp.int32),
+            pltpu.VMEM((columns, 128), jnp.int32),
+            pltpu.SMEM((columns, 128), jnp.int32),
             buf(slots, width),
             pltpu.VMEM((blocks, side), jnp.int32),
             pltpu.VMEM((columns, side), jnp.int32),
@@ -440,12 +426,11 @@
             buf(4, slots, width),
             buf(4, slots, width),
             pltpu.VMEM((4, slots, width), F32),
-            buf(4, half, width),
-            buf(4, half, width),
-            buf(3, half, width),
-            buf(3, half, width),
             buf(slots, width),
-            dma(6),
+            buf(slots, width),
+            buf(3, slots, width),
+            buf(3, slots, width),
+            dma(10),
             dma(1),
             dma(1),
             dma(3),
@@ -462,19 +447,19 @@
             dma(8),
             dma(4),
             dma(4),
-            dma(4),
-            dma(4),
+            dma(1),
+            dma(1),
             dma(3),
             dma(3),
-            dma(1),
-            dma(1),
         ],
         compiler_params=pltpu.CompilerParams(
             collective_id=0, has_side_effects=True, vmem_limit_bytes=60 * 1024 * 1024
         ),
         name="spiking_ffn",
     )(
-        table,
+        seq_lengths,
+        gateup_blocks,
+        down_blocks,
         tokens,
         in_exponents.reshape(blocks, side),
         hidden_exponents.reshape(columns, side),

time: 56.7 us -> 50.9 us (0.90)
  Pallas kernels: 52.7 us -> 49.2 us
  local copies, waits for them, and re-layouts: 2.98 us -> 1.47 us
  other arithmetic: 0.76 us -> 0 us
    pallas_call x1, Pallas kernels: 52.7 us -> 49.2 us  [local_kernel(): pl.pallas_call(body, out_shape=jax.ShapeDtypeStruct((slots, width), BF16)...]
    dynamic_slice x1 -> x0, local copies, waits for them, and re-layouts: 0.77 us -> none  [local_kernel(): lax.dynamic_slice_in_dim(gateup_blocks, t * kk, kk, axis=1)]
    concatenate x1 -> x0, local copies, waits for them, and re-layouts: 0.73 us -> none  [local_kernel(): jnp.concatenate([slot_of, lax.dynamic_slice_in_dim(gateup_blocks, t * kk,...]
    concatenate x1 -> x0, other arithmetic: 0.67 us -> none  [local_kernel(): jnp.concatenate([slot_of, lax.dynamic_slice_in_dim(gateup_blocks, t * kk,...]
where the time goes in v3:
time: 50.9 us; the launch traced here: 50.7 us
  Pallas kernels  49.2 us (97%)
  local copies, waits for them, and re-layouts  1.47 us (3%)
    pallas_call x1, Pallas kernels, local_kernel(): pl.pallas_call(body, out_shape=jax.ShapeDtypeStruct((slots, width), BF16)...  49.2 us
    unnamed x1, local copies, waits for them, and re-layouts  1.47 us

profile of v3, /device:TPU:0, one launch (start us, length us, event | category | flops | bytes accessed | tf_op | source)
XLA Modules:
  0.0 50.7 jit_solution(11502487622627988505)
XLA Ops:
  0.0 49.2 %spiking_ffn.1 = bf16[128,256]{1,0:T(8,128)(2,1)} custom-call(s32[4]{0:T(128)} %lengths_hbm.1, s32[8,16]{1,0:T(8,128)} %gateup_hbm.1, s32[8,16]{1,0:T(8,128)} %held_hbm.1, bf16[128,256]{1,0:T(8,128)(2,1)} %tok_hbm.1, s32[32,128]{1,0:T(8,128)} %bitcast.6, s32[8,128]{1,0:T(8,128)} %bitcast.7, bf16[8,1024,128]{2,1,0:T(8,128)(2,1)} %bitcast.4, ...), custom_call_target="tpu_custom_call" | custom-call | tf_op jit(solution)/shard_map/spiking_ffn/pallas_call | solution.py:398
  49.2 1.5 %copy.11 = bf16[128,256]{1,0:T(8,128)(2,1)} copy(bf16[128,256]{1,0:T(8,128)(2,1)} %spiking_ffn.1) | data formatting | bytes 131072

commit v4 on v3

--- a/solution.py
+++ b/solution.py
@@ -67,6 +67,13 @@
     rcv_y,
     snd_z,
     rcv_z,
+    snd_yr,
+    rcv_yr,
+    snd_xr,
+    rcv_xr,
+    snd_zr,
+    rcv_zr,
+    final,
     w_sem,
     raw_s,
     raw_r,
@@ -88,6 +95,10 @@
     y_r,
     z_s,
     z_r,
+    yr_s,
+    yr_r,
+    xr_s,
+    xr_r,
 ):
     t = lax.axis_index("tok")
     f = lax.axis_index("feat")
@@ -308,8 +319,19 @@
     def core_copy(i):
         return send(snd_c.at[i], rcv_c.at[i], c_s.at[i], c_r.at[i], dev_c)
 
+    half = live // 2
+    my_rows = pl.ds(pl.multiple_of(t * half, half), half)
+    peer_rows = pl.ds(pl.multiple_of((1 - t) * half, half), half)
+    front, back = pl.ds(0, width // 2), pl.ds(width // 2, width // 2)
+
     def x_copy(i):
         return send(snd_x.at[i], rcv_x.at[i], x_s.at[i], x_r.at[i], dev_x)
+
+    def y_rows_copy(i):
+        return send(snd_yr.at[i], rcv_yr.at[i], yr_s.at[i], yr_r.at[i], dev_y)
+
+    def x_rows_copy(i):
+        return send(snd_xr.at[i], rcv_xr.at[i], xr_s.at[i], xr_r.at[i], dev_x)
 
     def give_core_far(i, carry):
         snd_c[i] = down_chunk(chunk(z_turn(i), 1 - x, 1 - c)).astype(BF16)
@@ -324,42 +346,72 @@
     def give_x(i, carry):
         own = down_chunk(chunk(z_turn(i), 1 - x, c))
         core_copy(i).wait_recv()
-        snd_x[i] = (own + rcv_c[i].astype(F32)).astype(BF16)
+        acc[i] = own + rcv_c[i].astype(F32)
+        snd_x[i] = acc[i, :, front].astype(BF16)
         x_copy(i).start()
+        snd_yr[i] = acc[i, peer_rows, back].astype(BF16)
+        y_rows_copy(i).start()
         return carry
 
     def keep(i, carry):
         own = down_chunk(chunk(z_turn(i), x, c))
         core_copy(4 + i).wait_recv()
-        acc[i] = own + rcv_c[4 + i].astype(F32)
+        acc[4 + i] = own + rcv_c[4 + i].astype(F32)
+        snd_yr[4 + i] = acc[4 + i, peer_rows, back].astype(BF16)
+        y_rows_copy(4 + i).start()
+        return carry
+
+    def give_x_rows(i, carry):
+        y_rows_copy(i).wait_recv()
+        snd_xr[i] = (acc[i, my_rows, back] + rcv_yr[i].astype(F32)).astype(BF16)
+        x_rows_copy(i).start()
         return carry
 
     lax.fori_loop(0, 4, give_core_far, 0)
     lax.fori_loop(0, 4, give_x, 0)
     lax.fori_loop(0, 4, give_core_near, 0)
     lax.fori_loop(0, 4, keep, 0)
-
-    def own_sum(i):
+    lax.fori_loop(0, 4, give_x_rows, 0)
+
+    def front_sum(i):
         x_copy(i).wait_recv()
-        return acc[i] + rcv_x[i].astype(F32)
+        return acc[4 + i, :, front] + rcv_x[i].astype(F32)
+
+    def back_sum(i):
+        y_rows_copy(4 + i).wait_recv()
+        x_rows_copy(i).wait_recv()
+        return acc[4 + i, my_rows, back] + rcv_yr[4 + i].astype(F32) + rcv_xr[i].astype(F32)
+
+    def to_z(src, dst, n, d):
+        return start(send(src.at[d - 1], dst.at[d - 1], z_s.at[n], z_r.at[n], dev_z(d)))
 
     zs = []
+    zrs = []
     for i, d in enumerate((2, 3, 1)):
-        snd_z[d - 1] = own_sum(i).astype(BF16)
-        zs.append(
-            start(send(snd_z.at[d - 1], rcv_z.at[d - 1], z_s.at[d - 1], z_r.at[d - 1], dev_z(d)))
-        )
-    total = own_sum(3)
+        snd_z[d - 1] = front_sum(i).astype(BF16)
+        zs.append(to_z(snd_z, rcv_z, d - 1, d))
+    front_total = front_sum(3)
+    for i, d in enumerate((2, 3, 1)):
+        snd_zr[d - 1] = back_sum(i).astype(BF16)
+        zrs.append(to_z(snd_zr, rcv_zr, 2 + d, d))
+    back_total = back_sum(3)
     for copy, d in zip(zs, (2, 3, 1)):
         copy.wait_recv()
-        total = total + rcv_z[d - 1].astype(F32)
-    snd_y[...] = total.astype(BF16)
+        front_total = front_total + rcv_z[d - 1].astype(F32)
+    snd_y[...] = front_total.astype(BF16)
     fin = start(send(snd_y, rcv_y, y_s.at[0], y_r.at[0], dev_y))
+    for copy, d in zip(zrs, (2, 3, 1)):
+        copy.wait_recv()
+        back_total = back_total + rcv_zr[d - 1].astype(F32)
+    final[my_rows, :] = back_total.astype(BF16)
+    fin_rows = start(send(final.at[my_rows], final.at[my_rows], y_s.at[1], y_r.at[1], dev_y))
     slot_rows = lax.broadcasted_iota(jnp.int32, (slots, live), 0) + t * slots
     live_lanes = lax.broadcasted_iota(jnp.int32, (slots, live), 1)
     place = jnp.where(slot_target(lengths, slot_rows, side) == live_lanes, 1.0, 0.0).astype(BF16)
     fin.wait_recv()
-    result = (total + rcv_y[...].astype(F32)).astype(BF16)
+    front_part = (front_total + rcv_y[...].astype(F32)).astype(BF16)
+    fin_rows.wait_recv()
+    result = jnp.concatenate([front_part, final[...]], axis=1)
     out_ref[...] = jnp.dot(place, result, preferred_element_type=F32).astype(BF16)
 
     for copy in sent:
@@ -369,8 +421,10 @@
         rate_copy(i).wait_send()
     for i in range(8):
         core_copy(i).wait_send()
+        y_rows_copy(i).wait_send()
     for i in range(4):
         x_copy(i).wait_send()
+        x_rows_copy(i).wait_send()
 
 
 def local_kernel(
@@ -423,13 +477,20 @@
             buf(columns, slots, side),
             buf(8, slots, width),
             buf(8, slots, width),
-            buf(4, slots, width),
-            buf(4, slots, width),
-            pltpu.VMEM((4, slots, width), F32),
-            buf(slots, width),
-            buf(slots, width),
-            buf(3, slots, width),
-            buf(3, slots, width),
+            buf(4, slots, width // 2),
+            buf(4, slots, width // 2),
+            pltpu.VMEM((8, slots, width), F32),
+            buf(slots, width // 2),
+            buf(slots, width // 2),
+            buf(3, slots, width // 2),
+            buf(3, slots, width // 2),
+            buf(8, slots // 2, width // 2),
+            buf(8, slots // 2, width // 2),
+            buf(4, slots // 2, width // 2),
+            buf(4, slots // 2, width // 2),
+            buf(3, slots // 2, width // 2),
+            buf(3, slots // 2, width // 2),
+            buf(slots, width // 2),
             dma(10),
             dma(1),
             dma(1),
@@ -447,10 +508,14 @@
             dma(8),
             dma(4),
             dma(4),
-            dma(1),
-            dma(1),
-            dma(3),
-            dma(3),
+            dma(2),
+            dma(2),
+            dma(6),
+            dma(6),
+            dma(8),
+            dma(8),
+            dma(4),
+            dma(4),
         ],
         compiler_params=pltpu.CompilerParams(
             collective_id=0, has_side_effects=True, vmem_limit_bytes=60 * 1024 * 1024

time: 50.9 us -> 50.4 us (level)
  no operation moved by 1% of the time
where the time goes in v4:
time: 50.4 us; the launch traced here: 50.2 us
  Pallas kernels  48.7 us (97%)
  local copies, waits for them, and re-layouts  1.47 us (3%)
    pallas_call x1, Pallas kernels, local_kernel(): pl.pallas_call(body, out_shape=jax.ShapeDtypeStruct((slots, width), BF16)...  48.7 us
    unnamed x1, local copies, waits for them, and re-layouts  1.47 us

profile of v4, /device:TPU:0, one launch (start us, length us, event | category | flops | bytes accessed | tf_op | source)
XLA Modules:
  0.0 50.2 jit_solution(15241616999274846416)
XLA Ops:
  0.0 48.7 %spiking_ffn.1 = bf16[128,256]{1,0:T(8,128)(2,1)} custom-call(s32[4]{0:T(128)} %lengths_hbm.1, s32[8,16]{1,0:T(8,128)} %gateup_hbm.1, s32[8,16]{1,0:T(8,128)} %held_hbm.1, bf16[128,256]{1,0:T(8,128)(2,1)} %tok_hbm.1, s32[32,128]{1,0:T(8,128)} %bitcast.6, s32[8,128]{1,0:T(8,128)} %bitcast.7, bf16[8,1024,128]{2,1,0:T(8,128)(2,1)} %bitcast.4, ...), custom_call_target="tpu_custom_call" | custom-call | tf_op jit(solution)/shard_map/spiking_ffn/pallas_call | solution.py:452
  48.7 1.5 %copy.11 = bf16[128,256]{1,0:T(8,128)(2,1)} copy(bf16[128,256]{1,0:T(8,128)(2,1)} %spiking_ffn.1) | data formatting | bytes 131072

commit v5 on v4

--- a/solution.py
+++ b/solution.py
@@ -99,6 +99,8 @@
     yr_r,
     xr_s,
     xr_r,
+    agy_s,
+    agy_r,
 ):
     t = lax.axis_index("tok")
     f = lax.axis_index("feat")
@@ -213,15 +215,25 @@
     def forward_c(d, g):
         return start(send(all_tok.at[g], all_tok.at[g], agc_s.at[d], agc_r.at[d], dev_c))
 
+    half = live // 2
+    my_rows = pl.ds(pl.multiple_of(t * half, half), half)
+
+    def half_copy(g, ssem, rsem, dev):
+        return start(send(all_tok.at[g, my_rows], all_tok.at[g, my_rows], ssem, rsem, dev))
+
     z_copies = [
-        start(send(all_tok.at[f], all_tok.at[f], agz_s.at[d - 1], agz_r.at[d - 1], dev_z(d)))
-        for d in (1, 2, 3)
+        half_copy(f, agz_s.at[d - 1], agz_r.at[d - 1], dev_z(d)) for d in (1, 2, 3)
     ]
     x_copies = [forward_x(0, f)]
     c_copies = [forward_c(0, f)]
     rotate_low(f)
+    y_copies = []
     for d in (1, 3, 2):
         z_copies[d - 1].wait_recv()
+        g = chunk(z_at(4 - d), x, c)
+        y_copies.append(half_copy(g, agy_s.at[d - 1], agy_r.at[d - 1], dev_y))
+    for i, d in enumerate((1, 3, 2)):
+        y_copies[i].wait_recv()
         g = chunk(z_at(4 - d), x, c)
         x_copies.append(forward_x(d, g))
         c_copies.append(forward_c(d, g))
@@ -319,8 +331,6 @@
     def core_copy(i):
         return send(snd_c.at[i], rcv_c.at[i], c_s.at[i], c_r.at[i], dev_c)
 
-    half = live // 2
-    my_rows = pl.ds(pl.multiple_of(t * half, half), half)
     peer_rows = pl.ds(pl.multiple_of((1 - t) * half, half), half)
     front, back = pl.ds(0, width // 2), pl.ds(width // 2, width // 2)
 
@@ -516,6 +526,8 @@
             dma(8),
             dma(4),
             dma(4),
+            dma(3),
+            dma(3),
         ],
         compiler_params=pltpu.CompilerParams(
             collective_id=0, has_side_effects=True, vmem_limit_bytes=60 * 1024 * 1024

time: 50.4 us -> 52.1 us (1.034)
  Pallas kernels: 48.7 us -> 50.4 us
    pallas_call x1, Pallas kernels: 48.7 us -> 50.4 us  [local_kernel(): pl.pallas_call(body, out_shape=jax.ShapeDtypeStruct((slots, width), BF16)...]
where the time goes in v5:
time: 52.1 us; the launch traced here: 51.9 us
  Pallas kernels  50.4 us (97%)
  local copies, waits for them, and re-layouts  1.47 us (3%)
    pallas_call x1, Pallas kernels, local_kernel(): pl.pallas_call(body, out_shape=jax.ShapeDtypeStruct((slots, width), BF16)...  50.4 us
    unnamed x1, local copies, waits for them, and re-layouts  1.47 us

profile of v5, /device:TPU:0, one launch (start us, length us, event | category | flops | bytes accessed | tf_op | source)
XLA Modules:
  0.0 51.9 jit_solution(8162985830035774899)
XLA Ops:
  0.0 50.4 %spiking_ffn.1 = bf16[128,256]{1,0:T(8,128)(2,1)} custom-call(s32[4]{0:T(128)} %lengths_hbm.1, s32[8,16]{1,0:T(8,128)} %gateup_hbm.1, s32[8,16]{1,0:T(8,128)} %held_hbm.1, bf16[128,256]{1,0:T(8,128)(2,1)} %tok_hbm.1, s32[32,128]{1,0:T(8,128)} %bitcast.6, s32[8,128]{1,0:T(8,128)} %bitcast.7, bf16[8,1024,128]{2,1,0:T(8,128)(2,1)} %bitcast.4, ...), custom_call_target="tpu_custom_call" | custom-call | tf_op jit(solution)/shard_map/spiking_ffn/pallas_call | solution.py:462
  50.4 1.5 %copy.11 = bf16[128,256]{1,0:T(8,128)(2,1)} copy(bf16[128,256]{1,0:T(8,128)(2,1)} %spiking_ffn.1) | data formatting | bytes 131072

commit v6 on v4

--- a/solution.py
+++ b/solution.py
@@ -367,9 +367,14 @@
         x_rows_copy(i).start()
         return carry
 
-    lax.fori_loop(0, 4, give_core_far, 0)
-    lax.fori_loop(0, 4, give_x, 0)
-    lax.fori_loop(0, 4, give_core_near, 0)
+    def far_then_x(i, carry):
+        return give_x(i - 1, give_core_far(i, carry))
+
+    give_core_far(0, 0)
+    lax.fori_loop(1, 4, far_then_x, 0)
+    give_core_near(0, 0)
+    give_x(3, 0)
+    lax.fori_loop(1, 4, give_core_near, 0)
     lax.fori_loop(0, 4, keep, 0)
     lax.fori_loop(0, 4, give_x_rows, 0)
 

time: 50.4 us -> 51.4 us (1.020)
  Pallas kernels: 48.7 us -> 49.8 us
    pallas_call x1, Pallas kernels: 48.7 us -> 49.8 us  [local_kernel(): pl.pallas_call(body, out_shape=jax.ShapeDtypeStruct((slots, width), BF16)...]
where the time goes in v6:
time: 51.4 us; the launch traced here: 51.2 us
  Pallas kernels  49.8 us (97%)
  local copies, waits for them, and re-layouts  1.47 us (3%)
    pallas_call x1, Pallas kernels, local_kernel(): pl.pallas_call(body, out_shape=jax.ShapeDtypeStruct((slots, width), BF16)...  49.8 us
    unnamed x1, local copies, waits for them, and re-layouts  1.47 us

profile of v6, /device:TPU:0, one launch (start us, length us, event | category | flops | bytes accessed | tf_op | source)
XLA Modules:
  0.0 51.2 jit_solution(14445204688528018608)
XLA Ops:
  0.0 49.8 %spiking_ffn.1 = bf16[128,256]{1,0:T(8,128)(2,1)} custom-call(s32[4]{0:T(128)} %lengths_hbm.1, s32[8,16]{1,0:T(8,128)} %gateup_hbm.1, s32[8,16]{1,0:T(8,128)} %held_hbm.1, bf16[128,256]{1,0:T(8,128)(2,1)} %tok_hbm.1, s32[32,128]{1,0:T(8,128)} %bitcast.6, s32[8,128]{1,0:T(8,128)} %bitcast.7, bf16[8,1024,128]{2,1,0:T(8,128)(2,1)} %bitcast.4, ...), custom_call_target="tpu_custom_call" | custom-call | tf_op jit(solution)/shard_map/spiking_ffn/pallas_call | solution.py:457
  49.8 1.5 %copy.11 = bf16[128,256]{1,0:T(8,128)(2,1)} copy(bf16[128,256]{1,0:T(8,128)(2,1)} %spiking_ffn.1) | data formatting | bytes 131072
